TPU v7x, 128 devices: a whole 4x4x4 slice. The times are simulated.
128 devices in a mesh: row: 16 (over z, y_hi, core), col: 8 (over x, y_lo).
Axes of the slice: x: 4, y: 4 (y_hi: 2, y_lo: 2; y = y_hi * 2 + y_lo), z: 4, core: 2. Of those that a mesh axis runs over, the one named last changes fastest.
Arguments:
- inverse_tiles: bfloat16 [24576, 24576], P('row', 'col'), may hold values from -6 to 6
- factor: bfloat16 [24576, 2048], P('row', 'col'), may hold values from -0.0390625 to 0.0390625
- block_mask: int32 [192, 16], replicated, may hold values 0 or 1
- diag_inverse: float32 [16, 128, 128], replicated, may hold values from -6 to 6
Outputs:
- off_block: bfloat16 [2048, 24576], P('col', 'row')
- diag_block: float32 [16, 128, 128], P('col')
All inputs are finite; a program needn't handle non-finite values.
Results may differ from a plain program's by a relative error of at most 0.012.
Values may be sent and summed in bfloat16 or wider, within the bound.
A program may use at most 128 MiB of HBM per device.

v0:
```python
import jax
import jax.numpy as jnp
from jax import lax
from jax.sharding import Mesh
from jax.sharding import PartitionSpec as P

COL = ("col_0", "col_1")


def whole_of(x, axes, dim):
    for axis in reversed(axes):
        x = lax.all_gather(x, axis, axis=dim, tiled=True)
    return x


def filled_up(lines, length):
    spare = -lines.shape[0] % length
    if not spare:
        return lines
    return jnp.concatenate([lines, jnp.zeros((spare, *lines.shape[1:]), lines.dtype)])


def broadcast_by_parts(x, axis, root):
    lines = jnp.where(lax.axis_index(axis) == root, x, jnp.zeros_like(x)).reshape(
        -1, *x.shape[1:][-1:]
    )
    padded = filled_up(lines, lax.axis_size(axis))
    own = lax.psum_scatter(padded, axis, scatter_dimension=0, tiled=True)
    return lax.all_gather(own, axis, axis=0, tiled=True)[: len(lines)].reshape(x.shape)


def sum_by_axis(x, axes, dim):
    if not axes:
        return x
    nearer = lax.psum_scatter(x, axes[0], scatter_dimension=dim, tiled=True)
    return sum_by_axis(nearer, axes[1:], dim)


def sent_to_all(x, axis):
    length = lax.axis_size(axis)
    return lax.all_to_all(jnp.broadcast_to(x[None], (length, *x.shape)), axis, 0, 0, tiled=True)


def taken_together(x, axis):
    return sent_to_all(x, axis).astype(jnp.float32).sum(axis=0)


def per_device(inverse_tiles, factor, block_mask, diag_inverse):
    rows_here, cols_here = factor.shape
    block_width = diag_inverse.shape[1]
    sup_here = cols_here // block_width
    blocks_here = rows_here // block_width
    row_index = lax.axis_index("row")
    col_index = lax.axis_index(COL)
    mask_here = lax.dynamic_slice(
        block_mask, (row_index * blocks_here, col_index * sup_here), (blocks_here, sup_here)
    )
    keep_mask = jnp.repeat(jnp.repeat(mask_here, block_width, 0), block_width, 1).astype(
        jnp.bfloat16
    )
    masked = factor * keep_mask
    full_rows = whole_of(masked, COL, 1)
    row_ratio = lax.axis_size("row") // lax.axis_size(COL)
    row_pieces = []
    for offset in range(row_ratio):
        row_pieces.append(broadcast_by_parts(full_rows, "row", row_ratio * col_index + offset))
    summed = jnp.zeros((full_rows.shape[1], rows_here), jnp.float32)
    for offset in range(row_ratio):
        columns = row_pieces[offset]
        inverse_part = inverse_tiles[:, offset * rows_here : (offset + 1) * rows_here]
        summed = summed + lax.dot_general(
            columns, inverse_part, (((0,), (1,)), ((), ())), preferred_element_type=jnp.float32
        )
    reduced = sum_by_axis(summed, COL, 0)
    left_factor = masked.astype(jnp.float32).reshape(rows_here, sup_here, block_width)
    right_product = reduced.reshape(sup_here, block_width, rows_here)
    partial_diag = jnp.einsum(
        "jbr,rja->jab", right_product, left_factor, precision=lax.Precision.HIGHEST
    )
    summed_diag = taken_together(partial_diag.astype(jnp.bfloat16), "row").astype(jnp.float32)
    own_diag = lax.dynamic_slice_in_dim(diag_inverse, col_index * sup_here, sup_here, 0)
    return ((-reduced).astype(jnp.bfloat16), own_diag + summed_diag)


def solution(mesh):
    finer = Mesh(mesh.devices.reshape(mesh.shape["row"], 4, 2), ("row", "col_0", "col_1"))
    in_specs = (P("row", COL), P("row", COL), P(), P())
    out_specs = (P(COL, "row"), P(COL, None, None))
    return jax.shard_map(
        per_device, mesh=finer, in_specs=in_specs, out_specs=out_specs, check_vma=False
    )
```

profile of v0, /device:TPU:1, one launch (start us, length us, event | category | flops | bytes accessed | tf_op | source)
XLA Modules:
  0.0 650.2 jit_solution(2144273733660245835)
XLA Ops:
  7.2 0.0 all-gather.5.cloned.1.call-start
  7.2 0.8 dynamic-slice_convert_fusion
  8.0 0.1 copy.8
  8.1 0.1 broadcast_in_dim.12
  8.2 1.9 broadcast_in_dim.13
  10.1 2.1 bitcast_multiply_fusion
  12.3 0.0 all-gather.7.cloned.1.call-start
  12.3 33.0 %all-gather.5.cloned.1.call-done = bf16[1536,512]{1,0:T(8,128)(2,1)} async-done(((bf16[1536,256]{1,0:T(8,128)(2,1)}), bf16[1536,512]{1,0:T(8,128)(2,1)}) %all-gather.5.cloned.1.call-update) | async-done | bytes 1572880 | tf_op jit(solution)/shard_map/all_gather | solution.py:12
  45.3 0.0 reduce-scatter.5.cloned.1.call-start
  45.4 68.2 %all-gather.7.cloned.1.call-done = bf16[1536,2048]{1,0:T(8,128)(2,1)} async-done(((bf16[1536,512]{1,0:T(8,128)(2,1)}), bf16[1536,2048]{1,0:T(8,128)(2,1)}) %all-gather.7.cloned.1.call-update) | async-done | bytes 6291472 | tf_op jit(solution)/shard_map/all_gather | solution.py:12
  113.6 8.2 %broadcast_select_fusion = (bf16[1536,2048]{1,0:T(8,128)(2,1)}, bf16[1536,2048]{1,0:T(8,128)(2,1)}) fusion(bf16[1536,2048]{1,0:T(8,128)(2,1)} %all-gather.7.cloned.1.call-done, pred[]{:T(512)S(6)} %eq.7, pred[]{:T(512)S(6)} %eq.6), kind=kLoop, calls=%fused_computation.1 | loop fusion | flops 6291456 | bytes 18874370 | tf_op jit(solution)/shard_map/jit(_where)/select_n | solution.py:24
  121.8 0.0 reduce-scatter.7.cloned.1.call-start
  121.8 0.5 reduce-scatter.7.cloned.1.call-update
  122.4 0.0 all-gather.9.cloned.1.call-start
  122.4 88.9 %reduce-scatter.5.cloned.1.call-done = bf16[96,2048]{1,0:T(8,128)(2,1)} async-done(((bf16[1536,2048]{1,0:T(8,128)(2,1)}), bf16[96,2048]{1,0:T(8,128)(2,1)}) %reduce-scatter.5.cloned.1.call-update) | async-done | bytes 393232 | tf_op jit(solution)/shard_map/reduce_scatter | solution.py:28
  211.4 93.1 %reduce-scatter.7.cloned.1.call-done = bf16[96,2048]{1,0:T(8,128)(2,1)} async-done(((bf16[1536,2048]{1,0:T(8,128)(2,1)}), bf16[96,2048]{1,0:T(8,128)(2,1)}) %reduce-scatter.7.cloned.1.call-update) | async-done | bytes 393232 | tf_op jit(solution)/shard_map/reduce_scatter | solution.py:28
  304.6 0.0 reduce-scatter.9.cloned.1.call-start
  304.6 66.8 %all-gather.9.cloned.1.call-done = bf16[1536,2048]{1,0:T(8,128)(2,1)} async-done(((bf16[96,2048]{1,0:T(8,128)(2,1)}), bf16[1536,2048]{1,0:T(8,128)(2,1)}) %all-gather.9.cloned.1.call-update) | async-done | bytes 6291472 | tf_op jit(solution)/shard_map/all_gather | solution.py:29
  371.4 16.1 %fusion.1 = f32[2048,1536]{1,0:T(8,128)} fusion(bf16[1536,2048]{1,0:T(8,128)(2,1)} %all-gather.9.cloned.1.call-done, bf16[1536,3072]{1,0:T(8,128)(2,1)} %param.4), kind=kOutput, calls=%fused_computation.4 | convolution fusion | flops 9663676416 | bytes 23592960 | tf_op jit(solution)/shard_map/dot_general | solution.py:71
  387.5 48.2 %all-gather.11.cloned.1.call-done = bf16[1536,2048]{1,0:T(8,128)(2,1)} async-done(((bf16[96,2048]{1,0:T(8,128)(2,1)}), bf16[1536,2048]{1,0:T(8,128)(2,1)}) %all-gather.11.cloned.1.call-update) | async-done | bytes 6291472 | tf_op jit(solution)/shard_map/all_gather | solution.py:29
  435.7 17.9 %convolution_add_fusion = f32[2048,1536]{1,0:T(8,128)} fusion(f32[2048,1536]{1,0:T(8,128)} %fusion.1, bf16[1536,2048]{1,0:T(8,128)(2,1)} %all-gather.11.cloned.1.call-done, bf16[1536,3072]{1,0:T(8,128)(2,1)} %param.4), kind=kOutput, calls=%fused_computation | convolution fusion | flops 9666822144 | bytes 36175872 | tf_op jit(solution)/shard_map/dot_general | solution.py:71
  453.7 0.0 reduce-scatter.11.cloned.1.call-start
  453.7 111.8 %reduce-scatter.9.cloned.1.call-done = f32[512,1536]{1,0:T(8,128)} async-done(((f32[2048,1536]{1,0:T(8,128)}), f32[512,1536]{1,0:T(8,128)}) %reduce-scatter.9.cloned.1.call-update) | async-done | bytes 3145744 | tf_op jit(solution)/shard_map/reduce_scatter | solution.py:35
  565.6 0.3 copy.10
  565.9 47.6 %reduce-scatter.11.cloned.1.call-done = f32[256,1536]{1,0:T(8,128)} async-done(((f32[512,1536]{1,0:T(8,128)}), f32[256,1536]{1,0:T(8,128)}) %reduce-scatter.11.cloned.1.call-update) | async-done | bytes 1572880 | tf_op jit(solution)/shard_map/reduce_scatter | solution.py:35
  613.5 2.4 convolution_convert_fusion
  616.0 1.2 broadcast_in_dim.14
  617.2 7.3 %all-to-all-start = ((bf16[16,2,128,128]{3,2,1,0:T(8,128)(2,1)}), bf16[16,2,128,128]{3,2,1,0:T(8,128)(2,1)S(1)}, u32[]{:S(2)}, u32[]{:S(2)}) async-start(bf16[16,2,128,128]{3,2,1,0:T(8,128)(2,1)} %broadcast_in_dim.14), calls=%async_computation.4 | async-start | bytes 2097152 | tf_op jit(solution)/shard_map/all_to_all | solution.py:41
  624.5 1.0 negate_convert_fusion
  625.4 16.2 %all-to-all-done = bf16[16,2,128,128]{3,2,1,0:T(8,128)(2,1)S(1)} async-done(((bf16[16,2,128,128]{3,2,1,0:T(8,128)(2,1)}), bf16[16,2,128,128]{3,2,1,0:T(8,128)(2,1)S(1)}, u32[]{:S(2)}, u32[]{:S(2)}) %all-to-all-start) | async-done | bytes 1048608 | tf_op jit(solution)/shard_map/all_to_all | solution.py:41
  641.7 0.1 convert_reduce_fusion
  641.8 1.6 dynamic-slice_add_fusion
  (12 shorter events, 0.2 us)
Async XLA Ops:
  7.2 38.1 %all-gather.5.cloned.1.call-start = ((), (), s32[]{:S(2)}) async-start(), calls=%async_computation.5 | async-start | bytes 2359296 | tf_op jit(solution)/shard_map/all_gather | solution.py:12
  12.3 101.3 %all-gather.7.cloned.1.call-start = ((), (), s32[]{:S(2)}) async-start(), calls=%async_computation.6 | async-start | bytes 7864320 | tf_op jit(solution)/shard_map/all_gather | solution.py:12
  45.3 166.0 %reduce-scatter.5.cloned.1.call-start = ((), (), s32[]{:S(2)}) async-start(), calls=%async_computation.7 | async-start | bytes 6684672 | tf_op jit(solution)/shard_map/reduce_scatter | solution.py:28
  121.8 182.8 %reduce-scatter.7.cloned.1.call-start = ((), (), s32[]{:S(2)}) async-start(), calls=%async_computation.9 | async-start | bytes 6684672 | tf_op jit(solution)/shard_map/reduce_scatter | solution.py:28
  122.4 249.1 %all-gather.9.cloned.1.call-start = ((), (), s32[]{:S(2)}) async-start(), calls=%async_computation.8 | async-start | bytes 6684672 | tf_op jit(solution)/shard_map/all_gather | solution.py:29
  211.4 224.4 %all-gather.11.cloned.1.call-start = ((), (), s32[]{:S(2)}) async-start(), calls=%async_computation.10 | async-start | bytes 6684672 | tf_op jit(solution)/shard_map/all_gather | solution.py:29
  304.6 261.0 %reduce-scatter.9.cloned.1.call-start = ((), (), s32[]{:S(2)}) async-start(), calls=%async_computation.11 | async-start | bytes 15728640 | tf_op jit(solution)/shard_map/reduce_scatter | solution.py:35
  453.6 112.0 %copy-start = (bf16[1536,256]{1,0:T(8,128)(2,1)S(1)}, bf16[1536,256]{1,0:T(8,128)(2,1)}, u32[]{:S(2)}) copy-start(bf16[1536,256]{1,0:T(8,128)(2,1)} %bitcast_multiply_fusion) | copy-start | bytes 2359300
  453.7 159.8 %reduce-scatter.11.cloned.1.call-start = ((), (), s32[]{:S(2)}) async-start(), calls=%async_computation.12 | async-start | bytes 4718592 | tf_op jit(solution)/shard_map/reduce_scatter | solution.py:35
  613.5 10.9 %copy-start.1 = (f32[256,1536]{1,0:T(8,128)S(1)}, f32[256,1536]{1,0:T(8,128)}, u32[]{:S(2)}) copy-start(f32[256,1536]{1,0:T(8,128)} %reduce-scatter.11.cloned.1.call-done) | copy-start | bytes 4718596
  617.2 24.5 %all-to-all-start = ((bf16[16,2,128,128]{3,2,1,0:T(8,128)(2,1)}), bf16[16,2,128,128]{3,2,1,0:T(8,128)(2,1)S(1)}, u32[]{:S(2)}, u32[]{:S(2)}) async-start(bf16[16,2,128,128]{3,2,1,0:T(8,128)(2,1)} %broadcast_in_dim.14), calls=%async_computation.4 | async-start | bytes 2097152 | tf_op jit(solution)/shard_map/all_to_all | solution.py:41
Sparse Core Ops, SparseCore 0:
  12.4 32.8 all-gather.4
  47.0 66.5 all-gather.6
  121.9 89.3 reduce-scatter.4
  216.0 88.5 reduce-scatter.6
  306.8 64.5 all-gather.8
  373.8 61.9 all-gather.10
  453.8 111.7 reduce-scatter.8
  567.9 45.5 reduce-scatter.10
where the time goes:
time: 651 us; the launch traced here: 650 us
  waiting for transfers between devices  575 us (88%)
  matrix products  36.4 us (6%)
  between operations  14.2 us (2%)
  other arithmetic  13.8 us (2%)
  starting transfers between devices  7.6 us (1%)
    reduce_scatter x2, waiting for transfers between devices, broadcast_by_parts(): own = lax.psum_scatter(padded, axis, scatter_dimension=0, tiled=True)  182 us
    reduce_scatter x2, waiting for transfers between devices, sum_by_axis(): nearer = lax.psum_scatter(x, axes[0], scatter_dimension=dim, tiled=True)  159 us
    all_gather x2, waiting for transfers between devices, broadcast_by_parts(): lax.all_gather(own, axis, axis=0, tiled=True)[:len(lines)].reshape(x.shape)  115 us
    all_gather x2, waiting for transfers between devices, whole_of(): x = lax.all_gather(x, axis, axis=dim, tiled=True)  101 us
    dot_general x2, matrix products, per_device(): lax.dot_general(columns, inverse_part, (((0,), (1,)), ((), ())), preferre...  34 us
    all_to_all x1, waiting for transfers between devices, sent_to_all(): lax.all_to_all(jnp.broadcast_to(x[None], (length, *x.shape)), axis, 0, 0,...  16.2 us
  transfers between devices with their start and end apart: 9, of which 9 were waited for; matrix products, arithmetic and copies ran while one was open for 3% of the time, Pallas kernels for 0%

commit v1 on v0

v1 whole, which is shorter than its diff:
```python
import jax
import jax.numpy as jnp
from jax import lax
from jax.experimental import pallas as pl
from jax.experimental.pallas import tpu as pltpu
from jax.sharding import PartitionSpec as P

MESH = pl.DeviceIdType.MESH
BF = jnp.bfloat16
F32 = jnp.float32
W = 128
SLOTS = 2
PARTS = 3
STEPS = SLOTS * PARTS

T, Y, ZRO, ZLO, ZRP, ZLP, RR, RL = range(8)
SIB = 8
GATHER = 16
QR, QL, FR0, FR1, FL0, FL1, YL = range(7)
REDUCE = 7


def kernel(
    fac, a_hbm, mask, dinv_hbm, off, diag,
    a, dinv, masked, x, part, own, relay, fin, ysend, yrecv, dacc, dsend, drecv, dsum, dall,
    local_sem, g_send, g_recv, r_send, r_recv, d_send, d_recv,
):
    rows = fac.shape[0]
    slice_rows = rows // PARTS
    row, col = lax.axis_index("row"), lax.axis_index("col")
    z, yh, p = row // 4, (row // 2) % 2, row % 2
    xi, yl = col // 2, col % 2
    zr, zl, z2 = (z + 1) % 4, (z + 3) % 4, (z + 2) % 4
    xr, xl, x2 = (xi + 1) % 4, (xi + 3) % 4, (xi + 2) % 4

    def dev(z_, yh_, p_, x_, yl_):
        return (z_ * 4 + yh_ * 2 + p_, x_ * 2 + yl_)

    turned = dev(xi, yl, p, z, yh)
    at_home = jnp.logical_and(xi == z, yl == yh)
    partner = dev(z, 1 - yh, p, xi, yl)
    z_right, z_left = dev(zr, yh, p, xi, yl), dev(zl, yh, p, xi, yl)
    sibling = dev(z, yh, 1 - p, xi, yl)
    x_right, x_left = dev(z, yh, p, xr, yl), dev(z, yh, p, xl, yl)
    y_near = dev(z, yh, p, xi, 1 - yl)

    a_copy = pltpu.make_async_copy(a_hbm, a, local_sem.at[0])
    a_copy.start()
    dinv_copy = pltpu.make_async_copy(dinv_hbm.at[pl.ds(col * 16, 16)], dinv, local_sem.at[1])
    dinv_copy.start()

    barrier = pltpu.get_barrier_semaphore()

    @pl.loop(1, 16)
    def _(o):
        pl.semaphore_signal(barrier, inc=1, device_id=((row + o) % 16, col), device_id_type=MESH)

    for d in (x_right, x_left, y_near):
        pl.semaphore_signal(barrier, inc=1, device_id=d, device_id_type=MESH)

    @pl.when(jnp.logical_not(at_home))
    def _():
        pl.semaphore_signal(barrier, inc=1, device_id=turned, device_id_type=MESH)

    for s in range(SLOTS):
        for b in range(rows // W):
            keep = mask[row * (rows // W) + b, col * SLOTS + s].astype(F32)
            block = fac[b * W : (b + 1) * W, s * W : (s + 1) * W].astype(F32)
            masked[s, b * W : (b + 1) * W, :] = (block * keep).astype(BF)

    pl.semaphore_wait(barrier, jnp.where(at_home, 18, 19))

    pending = []

    def remote(src, dst, send, recv, i, device):
        return pltpu.make_async_remote_copy(
            src_ref=src, dst_ref=dst, send_sem=send.at[i], recv_sem=recv.at[i],
            device_id=device, device_id_type=MESH,
        )

    k, kp = 2 * z + yh, 2 * z + 1 - yh
    lo, lp = 2 * zl + yh, 2 * zl + 1 - yh
    ro, rp = 2 * zr + yh, 2 * zr + 1 - yh
    fo, fp = 2 * z2 + yh, 2 * z2 + 1 - yh

    gcopies = {}

    def gather_copy(s, i, g, device):
        c = remote(x.at[s, p, g], x.at[s, p, g], g_send, g_recv, s * GATHER + i, device)
        gcopies[s, i] = c
        return c

    def start_gather(s, i, g, device):
        c = gather_copy(s, i, g, device)
        c.start()
        pending.append(c)

    def got(s, i):
        gcopies[s, i].wait_recv()

    def turn_copies(s):
        away = remote(masked.at[s], x.at[s, p, 2 * xi + yl], g_send, g_recv, s * GATHER + T, turned)
        here = pltpu.make_async_copy(masked.at[s], x.at[s, p, k], g_recv.at[s * GATHER + T])
        return away, here

    def start_turn(s):
        away, here = turn_copies(s)

        @pl.when(jnp.logical_not(at_home))
        def _():
            away.start()

        @pl.when(at_home)
        def _():
            here.start()

    def event0(s):
        away, here = turn_copies(s)

        @pl.when(jnp.logical_not(at_home))
        def _():
            away.wait_recv()
            away.wait_send()

        @pl.when(at_home)
        def _():
            here.wait()

        start_gather(s, ZRO, k, z_right)
        start_gather(s, ZLO, k, z_left)
        start_gather(s, Y, k, partner)
        start_gather(s, SIB + 0, k, sibling)

    def event1(s):
        got(s, Y)
        start_gather(s, ZRP, kp, z_right)
        start_gather(s, ZLP, kp, z_left)
        start_gather(s, SIB + 1, kp, sibling)

    def event2(s):
        got(s, ZRO)
        start_gather(s, RR, lo, z_right)
        start_gather(s, SIB + 2, lo, sibling)
        got(s, ZLO)
        start_gather(s, SIB + 3, ro, sibling)

    def event3(s):
        got(s, ZLP)
        start_gather(s, RL, rp, z_left)
        start_gather(s, SIB + 4, rp, sibling)
        got(s, ZRP)
        start_gather(s, SIB + 5, lp, sibling)

    def event4(s):
        got(s, RR)
        start_gather(s, SIB + 6, fo, sibling)
        got(s, RL)
        start_gather(s, SIB + 7, fp, sibling)

    def event5(s):
        for i in range(8):
            got(s, SIB + i)

    def product(t, dest):
        s, m = divmod(t, PARTS)
        here = slice(m * slice_rows, (m + 1) * slice_rows)
        total = None
        for half in range(2):
            right = jnp.concatenate([x[s, half, 2 * dest], x[s, half, 2 * dest + 1]], axis=1)
            term = jnp.dot(a[here, half * rows : (half + 1) * rows], right, preferred_element_type=F32)
            total = term if total is None else total + term
        return total

    rcopies = {}

    def start_reduce(t, i, src, dst, device):
        c = remote(src, dst, r_send, r_recv, t * REDUCE + i, device)
        c.start()
        rcopies[t, i] = c
        pending.append(c)

    def arrived(t, i):
        rcopies[t, i].wait_recv()

    def multiply(t):
        @pl.loop(0, 3)
        def _(j):
            block = product(t, (xi + 1 + j) % 4)
            part[t, j, 0] = block[:, :W].astype(BF)
            part[t, j, 1] = block[:, W:].astype(BF)

        start_reduce(t, QR, part.at[t, 1, 0], relay.at[t, 0], x_right)
        start_reduce(t, QL, part.at[t, 1, 1], relay.at[t, 1], x_left)
        start_reduce(t, FR1, part.at[t, 0, 1], fin.at[t, 0, 1], x_right)
        start_reduce(t, FL0, part.at[t, 2, 0], fin.at[t, 1, 0], x_left)
        block = product(t, xi)
        own[t, 0] = block[:, :W]
        own[t, 1] = block[:, W:]

    def pass_on(t):
        arrived(t, QR)
        part[t, 0, 0] = (part[t, 0, 0].astype(F32) + relay[t, 0].astype(F32)).astype(BF)
        start_reduce(t, FR0, part.at[t, 0, 0], fin.at[t, 0, 0], x_right)
        arrived(t, QL)
        part[t, 2, 1] = (part[t, 2, 1].astype(F32) + relay[t, 1].astype(F32)).astype(BF)
        start_reduce(t, FL1, part.at[t, 2, 1], fin.at[t, 1, 1], x_left)

    def finish(t):
        for i in (FR0, FR1, FL0, FL1):
            arrived(t, i)
        far = 1 - yl
        ysend[t] = (own[t, far] + fin[t, 0, far].astype(F32) + fin[t, 1, far].astype(F32)).astype(BF)
        start_reduce(t, YL, ysend.at[t], yrecv.at[t], y_near)
        own[t, yl] = own[t, yl] + fin[t, 0, yl].astype(F32) + fin[t, 1, yl].astype(F32)

    def put(t):
        s, m = divmod(t, PARTS)
        here = slice(m * slice_rows, (m + 1) * slice_rows)
        arrived(t, YL)
        turned_product = (own[t, yl] + yrecv[t].astype(F32)).T
        off[s * W : (s + 1) * W, here] = (-turned_product).astype(BF)
        high = turned_product.astype(BF)
        low = (turned_product - high.astype(F32)).astype(BF)
        right = masked[s, here, :]
        term = jnp.dot(high, right, preferred_element_type=F32) + jnp.dot(
            low, right, preferred_element_type=F32
        )
        if m == 0:
            dacc[s] = term
        else:
            dacc[s] += term

    start_turn(0)
    start_turn(1)
    event0(0)
    event1(0)
    event2(0)
    event3(0)
    event0(1)
    event4(0)
    event1(1)
    a_copy.wait()
    dinv_copy.wait()
    event5(0)
    multiply(0)
    event2(1)
    multiply(1)
    pass_on(0)
    event3(1)
    multiply(2)
    pass_on(1)
    finish(0)
    event4(1)
    pass_on(2)
    finish(1)
    put(0)
    event5(1)
    multiply(3)
    finish(2)
    put(1)
    multiply(4)
    pass_on(3)
    put(2)
    multiply(5)
    pass_on(4)
    finish(3)
    pass_on(5)
    finish(4)
    put(3)
    finish(5)
    put(4)
    put(5)

    for s in range(SLOTS):
        dsend[s * 8 : (s + 1) * 8] = dacc[s].T.reshape(8, 16, W)

    def scatter_copy(o):
        to = (row + o) % 16
        return remote(dsend.at[to], drecv.at[o], d_send, d_recv, o, (to, col))

    def spread_copy(o):
        to = (row + o) % 16
        return remote(dsum, dall.at[row], d_send, d_recv, 16 + o, (to, col))

    @pl.loop(1, 16)
    def _(o):
        scatter_copy(o).start()

    @pl.loop(1, 16)
    def _(o):
        scatter_copy(o).wait_recv()

    total = dsend[row] + dinv[row]
    for o in range(1, 16):
        total = total + drecv[o]
    dsum[...] = total

    @pl.loop(1, 16)
    def _(o):
        spread_copy(o).start()

    diag[row] = total

    @pl.loop(1, 16)
    def _(o):
        spread_copy(o).wait_recv()
        since = (row + 16 - o) % 16
        diag[since] = dall[since]

    @pl.loop(1, 16)
    def _(o):
        scatter_copy(o).wait_send()
        spread_copy(o).wait_send()

    for c in pending:
        c.wait_send()


def per_device(inverse_tiles, factor, block_mask, diag_inverse):
    rows, depth = inverse_tiles.shape
    cols = factor.shape[1]
    part_rows = rows // PARTS
    vmem = pl.BlockSpec(memory_space=pltpu.VMEM)
    anywhere = pl.BlockSpec(memory_space=pl.ANY)
    off, diag = pl.pallas_call(
        kernel,
        out_shape=(
            jax.ShapeDtypeStruct((cols, rows), BF),
            jax.ShapeDtypeStruct((16, 16, W), F32),
        ),
        in_specs=[vmem, anywhere, pl.BlockSpec(memory_space=pltpu.SMEM), anywhere],
        out_specs=(vmem, vmem),
        scratch_shapes=[
            pltpu.VMEM((rows, depth), BF),
            pltpu.VMEM((16, 16, W), F32),
            pltpu.VMEM((SLOTS, rows, W), BF),
            pltpu.VMEM((SLOTS, 2, 8, rows, W), BF),
            pltpu.VMEM((STEPS, 3, 2, part_rows, W), BF),
            pltpu.VMEM((STEPS, 2, part_rows, W), F32),
            pltpu.VMEM((STEPS, 2, part_rows, W), BF),
            pltpu.VMEM((STEPS, 2, 2, part_rows, W), BF),
            pltpu.VMEM((STEPS, part_rows, W), BF),
            pltpu.VMEM((STEPS, part_rows, W), BF),
            pltpu.VMEM((SLOTS, W, W), F32),
            pltpu.VMEM((16, 16, W), F32),
            pltpu.VMEM((16, 16, W), F32),
            pltpu.VMEM((16, W), F32),
            pltpu.VMEM((16, 16, W), F32),
            pltpu.SemaphoreType.DMA((2,)),
            pltpu.SemaphoreType.DMA((SLOTS * GATHER,)),
            pltpu.SemaphoreType.DMA((SLOTS * GATHER,)),
            pltpu.SemaphoreType.DMA((STEPS * REDUCE,)),
            pltpu.SemaphoreType.DMA((STEPS * REDUCE,)),
            pltpu.SemaphoreType.DMA((32,)),
            pltpu.SemaphoreType.DMA((32,)),
        ],
        compiler_params=pltpu.CompilerParams(
            collective_id=0, has_side_effects=True, vmem_limit_bytes=58 * 1024 * 1024
        ),
    )(factor, inverse_tiles, block_mask, diag_inverse.reshape(8 * 16, 16, W))
    return off, diag.reshape(2, W, W)


def solution(mesh):
    return jax.shard_map(
        per_device,
        mesh=mesh,
        in_specs=(P("row", "col"), P("row", "col"), P(), P()),
        out_specs=(P("col", "row"), P("col", None, None)),
        check_vma=False,
    )
```

time: 651 us -> 194 us (0.30)
  waiting for transfers between devices: 575 us -> 0 us
  Pallas kernels: 0 us -> 187 us
  matrix products: 36.4 us -> 0 us
  other arithmetic: 13.8 us -> 0 us
  between operations: 14.2 us -> 0.64 us
  starting transfers between devices: 7.6 us -> 0 us
    reduce_scatter x4 -> x0, waiting for transfers between devices: 342 us -> none  [the longest x2 182 us: broadcast_by_parts(): own = lax.psum_scatter(padded, axis, scatter_dimension=0, tiled=True)]
    all_gather x4 -> x0, waiting for transfers between devices: 216 us -> none  [the longest x2 115 us: broadcast_by_parts(): lax.all_gather(own, axis, axis=0, tiled=True)[:len(lines)].reshape(x.shape)]
    pallas_call x0 -> x1, Pallas kernels: none -> 187 us  [per_device(): pl.pallas_call(kernel, out_shape=(jax.ShapeDtypeStruct((cols, rows), BF),...]
    dot_general x3 -> x0, matrix products: 36.4 us -> none  [the longest x2 34 us: per_device(): lax.dot_general(columns, inverse_part, (((0,), (1,)), ((), ())), preferre...]
    all_to_all x1 -> x0, waiting for transfers between devices: 16.2 us -> none  [sent_to_all(): lax.all_to_all(jnp.broadcast_to(x[None], (length, *x.shape)), axis, 0, 0,...]
    select_n x1 -> x0, other arithmetic: 8.16 us -> none  [broadcast_by_parts(): jnp.where(lax.axis_index(axis) == root, x, jnp.zeros_like(x))]
    all_to_all x1 -> x0, starting transfers between devices: 7.28 us -> none  [sent_to_all(): lax.all_to_all(jnp.broadcast_to(x[None], (length, *x.shape)), axis, 0, 0,...]
  transfers between devices with their start and end apart: 9 -> 0, of which waited for: 9 -> 0; matrix products, arithmetic and copies ran while one was open for 3% -> 0% of each run, Pallas kernels for 0% -> 0%
where the time goes in v1:
time: 194 us; the launch traced here: 193 us
  Pallas kernels  187 us (96%)
  local copies, waits for them, and re-layouts  5.09 us (3%)
    pallas_call x1, Pallas kernels, per_device(): pl.pallas_call(kernel, out_shape=(jax.ShapeDtypeStruct((cols, rows), BF),...  187 us
    unnamed x3, local copies, waits for them, and re-layouts  5.09 us

profile of v1, /device:TPU:1, one launch (start us, length us, event | category | flops | bytes accessed | tf_op | source)
XLA Modules:
  0.0 193.1 jit_solution(11416999821362105720)
XLA Ops:
  0.6 1.5 copy.6.mask
  2.1 187.4 %shard_map.59 = (bf16[256,1536]{1,0:T(8,128)(2,1)}, f32[16,16,128]{2,1,0:T(8,128)}) custom-call(bf16[1536,256]{1,0:T(8,128)(2,1)} %fac.1, bf16[1536,3072]{1,0:T(8,128)(2,1)} %a_hbm.1, s32[192,16]{1,0:T(8,128)} %copy.6.mask, f32[128,16,128]{2,1,0:T(8,128)} %bitcast.2), custom_call_target="tpu_custom_call" | custom-call | tf_op jit(solution)/shard_map/pallas_call | solution.py:325
  189.5 2.1 %copy.9 = bf16[256,1536]{1,0:T(8,128)(2,1)} copy(bf16[256,1536]{1,0:T(8,128)(2,1)} %get-tuple-element.8) | data formatting | bytes 1572864
  191.5 1.6 copy.10

commit v2 on v1

--- a/solution.py
+++ b/solution.py
@@ -13,7 +13,7 @@
 PARTS = 3
 STEPS = SLOTS * PARTS
 
-T, Y, ZRO, ZLO, ZRP, ZLP, RR, RL = range(8)
+YA, YB, ZRO, ZLO, ZRP, ZLP, RR, RL = range(8)
 SIB = 8
 GATHER = 16
 QR, QL, FR0, FR1, FL0, FL1, YL = range(7)
@@ -22,8 +22,8 @@
 
 def kernel(
     fac, a_hbm, mask, dinv_hbm, off, diag,
-    a, dinv, masked, x, part, own, relay, fin, ysend, yrecv, dacc, dsend, drecv, dsum, dall,
-    local_sem, g_send, g_recv, r_send, r_recv, d_send, d_recv,
+    a, dinv, masked, x, hub, turned, part, own, relay, fin, ysend, yrecv, dacc, dsend, drecv, dsum, dall,
+    local_sem, g_send, g_recv, h_send, h_recv, f_send, t_recv, r_send, r_recv, d_send, d_recv,
 ):
     rows = fac.shape[0]
     slice_rows = rows // PARTS
@@ -36,9 +36,9 @@
     def dev(z_, yh_, p_, x_, yl_):
         return (z_ * 4 + yh_ * 2 + p_, x_ * 2 + yl_)
 
-    turned = dev(xi, yl, p, z, yh)
-    at_home = jnp.logical_and(xi == z, yl == yh)
-    partner = dev(z, 1 - yh, p, xi, yl)
+    on_diagonal = xi == z
+    moves_near = yl != yh
+    y_first, y_second = dev(z, yl, p, xi, yh), dev(z, 1 - yl, p, xi, yh)
     z_right, z_left = dev(zr, yh, p, xi, yl), dev(zl, yh, p, xi, yl)
     sibling = dev(z, yh, 1 - p, xi, yl)
     x_right, x_left = dev(z, yh, p, xr, yl), dev(z, yh, p, xl, yl)
@@ -55,12 +55,12 @@
     def _(o):
         pl.semaphore_signal(barrier, inc=1, device_id=((row + o) % 16, col), device_id_type=MESH)
 
-    for d in (x_right, x_left, y_near):
+    for d in (x_right, x_left, dev(z, yh, p, x2, yl), y_near):
         pl.semaphore_signal(barrier, inc=1, device_id=d, device_id_type=MESH)
 
-    @pl.when(jnp.logical_not(at_home))
+    @pl.when(moves_near)
     def _():
-        pl.semaphore_signal(barrier, inc=1, device_id=turned, device_id_type=MESH)
+        pl.semaphore_signal(barrier, inc=1, device_id=y_first, device_id_type=MESH)
 
     for s in range(SLOTS):
         for b in range(rows // W):
@@ -68,7 +68,7 @@
             block = fac[b * W : (b + 1) * W, s * W : (s + 1) * W].astype(F32)
             masked[s, b * W : (b + 1) * W, :] = (block * keep).astype(BF)
 
-    pl.semaphore_wait(barrier, jnp.where(at_home, 18, 19))
+    pl.semaphore_wait(barrier, jnp.where(moves_near, 20, 19))
 
     pending = []
 
@@ -98,41 +98,96 @@
     def got(s, i):
         gcopies[s, i].wait_recv()
 
-    def turn_copies(s):
-        away = remote(masked.at[s], x.at[s, p, 2 * xi + yl], g_send, g_recv, s * GATHER + T, turned)
-        here = pltpu.make_async_copy(masked.at[s], x.at[s, p, k], g_recv.at[s * GATHER + T])
+    halves = (slice(0, rows // 2), slice(rows // 2, rows))
+
+    def to_hub(s, h):
+        j = (xi - z + 4) % 4 if h == 0 else (z - xi + 4) % 4
+        device = dev(z, yh, p, z, yl) if h == 0 else dev(xi, yh, p, xi, yl)
+        i = (s * 2 + h) * 4
+        return pltpu.make_async_remote_copy(
+            src_ref=masked.at[s, halves[h]], dst_ref=hub.at[s, h, j],
+            send_sem=h_send.at[s * 2 + h], recv_sem=h_recv.at[i + j],
+            device_id=device, device_id_type=MESH,
+        )
+
+    def from_hub(s, h, j):
+        device = dev((z + j) % 4, yh, p, xi, yl) if h == 0 else dev(z, yh, p, (xi + j) % 4, yl)
+        i = (s * 2 + h) * 4
+        return pltpu.make_async_remote_copy(
+            src_ref=hub.at[s, h, j], dst_ref=turned.at[s, halves[h]],
+            send_sem=f_send.at[i + j], recv_sem=t_recv.at[s * 2 + h],
+            device_id=device, device_id_type=MESH,
+        )
+
+    def at_hub(s, h, j):
+        i = (s * 2 + h) * 4
+        return pltpu.make_async_copy(masked.at[s, halves[h]], hub.at[s, h, j], h_recv.at[i + j])
+
+    def stay(s, h):
+        return pltpu.make_async_copy(masked.at[s, halves[h]], turned.at[s, halves[h]], t_recv.at[s * 2 + h])
+
+    def start_turn(s):
+        for h in range(2):
+            @pl.when(jnp.logical_not(on_diagonal))
+            def _():
+                to_hub(s, h).start()
+
+            @pl.when(on_diagonal)
+            def _():
+                stay(s, h).start()
+
+    def pass_hub(s):
+        @pl.when(on_diagonal)
+        def _():
+            for j in (1, 3, 2):
+                for h in range(2):
+                    at_hub(s, h, j).wait()
+                    from_hub(s, h, j).start()
+
+    def end_turn(s):
+        for h in range(2):
+            stay(s, h).wait()
+
+    def end_hub():
+        for s in range(SLOTS):
+            for h in range(2):
+                @pl.when(jnp.logical_not(on_diagonal))
+                def _():
+                    to_hub(s, h).wait_send()
+
+                @pl.when(on_diagonal)
+                def _():
+                    for j in (1, 3, 2):
+                        from_hub(s, h, j).wait_send()
+
+    def near_copies(s):
+        away = remote(turned.at[s], x.at[s, p, 2 * z + yl], g_send, g_recv, s * GATHER + YA, y_first)
+        here = pltpu.make_async_copy(turned.at[s], x.at[s, p, k], g_recv.at[s * GATHER + YA])
         return away, here
 
-    def start_turn(s):
-        away, here = turn_copies(s)
-
-        @pl.when(jnp.logical_not(at_home))
+    def event0(s):
+        end_turn(s)
+        away, here = near_copies(s)
+
+        @pl.when(moves_near)
         def _():
             away.start()
 
-        @pl.when(at_home)
+        @pl.when(jnp.logical_not(moves_near))
         def _():
             here.start()
 
-    def event0(s):
-        away, here = turn_copies(s)
-
-        @pl.when(jnp.logical_not(at_home))
-        def _():
-            away.wait_recv()
-            away.wait_send()
-
-        @pl.when(at_home)
-        def _():
-            here.wait()
-
+        c = remote(turned.at[s], x.at[s, p, 2 * z + yl], g_send, g_recv, s * GATHER + YB, y_second)
+        c.start()
+        gcopies[s, YB] = c
+        pending.append(c)
+        here.wait()
         start_gather(s, ZRO, k, z_right)
         start_gather(s, ZLO, k, z_left)
-        start_gather(s, Y, k, partner)
         start_gather(s, SIB + 0, k, sibling)
 
     def event1(s):
-        got(s, Y)
+        got(s, YB)
         start_gather(s, ZRP, kp, z_right)
         start_gather(s, ZLP, kp, z_left)
         start_gather(s, SIB + 1, kp, sibling)
@@ -232,8 +287,10 @@
 
     start_turn(0)
     start_turn(1)
+    pass_hub(0)
     event0(0)
     event1(0)
+    pass_hub(1)
     event2(0)
     event3(0)
     event0(1)
@@ -314,6 +371,11 @@
 
     for c in pending:
         c.wait_send()
+    for s in range(SLOTS):
+        @pl.when(moves_near)
+        def _():
+            near_copies(s)[0].wait_send()
+    end_hub()
 
 
 def per_device(inverse_tiles, factor, block_mask, diag_inverse):
@@ -335,6 +397,8 @@
             pltpu.VMEM((16, 16, W), F32),
             pltpu.VMEM((SLOTS, rows, W), BF),
             pltpu.VMEM((SLOTS, 2, 8, rows, W), BF),
+            pltpu.VMEM((SLOTS, 2, 4, rows // 2, W), BF),
+            pltpu.VMEM((SLOTS, rows, W), BF),
             pltpu.VMEM((STEPS, 3, 2, part_rows, W), BF),
             pltpu.VMEM((STEPS, 2, part_rows, W), F32),
             pltpu.VMEM((STEPS, 2, part_rows, W), BF),
@@ -349,6 +413,10 @@
             pltpu.SemaphoreType.DMA((2,)),
             pltpu.SemaphoreType.DMA((SLOTS * GATHER,)),
             pltpu.SemaphoreType.DMA((SLOTS * GATHER,)),
+            pltpu.SemaphoreType.DMA((SLOTS * 2,)),
+            pltpu.SemaphoreType.DMA((SLOTS * 8,)),
+            pltpu.SemaphoreType.DMA((SLOTS * 8,)),
+            pltpu.SemaphoreType.DMA((SLOTS * 2,)),
             pltpu.SemaphoreType.DMA((STEPS * REDUCE,)),
             pltpu.SemaphoreType.DMA((STEPS * REDUCE,)),
             pltpu.SemaphoreType.DMA((32,)),

time: 194 us -> 164 us (0.85)
  Pallas kernels: 187 us -> 158 us
    pallas_call x1, Pallas kernels: 187 us -> 158 us  [per_device(): pl.pallas_call(kernel, out_shape=(jax.ShapeDtypeStruct((cols, rows), BF),...]
where the time goes in v2:
time: 164 us
  Pallas kernels  158 us (96%)
  local copies, waits for them, and re-layouts  5.09 us (3%)
    pallas_call x1, Pallas kernels, per_device(): pl.pallas_call(kernel, out_shape=(jax.ShapeDtypeStruct((cols, rows), BF),...  158 us
    unnamed x3, local copies, waits for them, and re-layouts  5.09 us

profile of v2, /device:TPU:1, one launch (start us, length us, event | category | flops | bytes accessed | tf_op | source)
XLA Modules:
  0.0 163.7 jit_solution(8131440476738866797)
XLA Ops:
  0.6 1.5 copy.6.mask
  2.1 158.0 %shard_map.59 = (bf16[256,1536]{1,0:T(8,128)(2,1)}, f32[16,16,128]{2,1,0:T(8,128)}) custom-call(bf16[1536,256]{1,0:T(8,128)(2,1)} %fac.1, bf16[1536,3072]{1,0:T(8,128)(2,1)} %a_hbm.1, s32[192,16]{1,0:T(8,128)} %copy.6.mask, f32[128,16,128]{2,1,0:T(8,128)} %bitcast.2), custom_call_target="tpu_custom_call" | custom-call | tf_op jit(solution)/shard_map/pallas_call | solution.py:387
  160.1 2.1 %copy.9 = bf16[256,1536]{1,0:T(8,128)(2,1)} copy(bf16[256,1536]{1,0:T(8,128)(2,1)} %get-tuple-element.8) | data formatting | bytes 1572864
  162.1 1.6 copy.10

commit v3 on v1

v3 whole, which is shorter than its diff:
```python
import jax
import jax.numpy as jnp
from jax import lax
from jax.experimental import pallas as pl
from jax.experimental.pallas import tpu as pltpu
from jax.sharding import PartitionSpec as P

MESH = pl.DeviceIdType.MESH
BF = jnp.bfloat16
F32 = jnp.float32
W = 128
HALVES = 2
SLOTS = 4
PARTS = 3
STEPS = SLOTS * PARTS

Y, ZR, ZL = 0, 2, 4
RR, RL = 6, 7
SIB = 8
GATHER = 16
QR, QL, FR0, FR1, FL0, FL1, YL = range(7)
REDUCE = 7


def kernel(
    fac, a_hbm, mask, dinv_hbm, off, diag,
    a, dinv, masked, x, hub, turned, part, own, relay, fin, ysend, yrecv, dacc, dsend, drecv, dsum, dall,
    local_sem, g_send, g_recv, y_send, h_send, h_recv, f_send, t_recv, r_send, r_recv, d_send, d_recv,
):
    rows = fac.shape[0]
    slice_rows = rows // PARTS
    row, col = lax.axis_index("row"), lax.axis_index("col")
    z, yh, p = row // 4, (row // 2) % 2, row % 2
    xi, yl = col // 2, col % 2
    zr, zl, z2 = (z + 1) % 4, (z + 3) % 4, (z + 2) % 4
    xr, xl, x2 = (xi + 1) % 4, (xi + 3) % 4, (xi + 2) % 4

    def dev(z_, yh_, p_, x_, yl_):
        return (z_ * 4 + yh_ * 2 + p_, x_ * 2 + yl_)

    on_diagonal = xi == z
    moves_near = yl != yh
    y_other = dev(z, yl, p, xi, yh)
    z_right, z_left = dev(zr, yh, p, xi, yl), dev(zl, yh, p, xi, yl)
    sibling = dev(z, yh, 1 - p, xi, yl)
    x_right, x_left = dev(z, yh, p, xr, yl), dev(z, yh, p, xl, yl)
    y_near = dev(z, yh, p, xi, 1 - yl)

    dacc[...] = jnp.zeros_like(dacc)
    a_copy = pltpu.make_async_copy(a_hbm, a, local_sem.at[0])
    a_copy.start()
    dinv_copy = pltpu.make_async_copy(dinv_hbm.at[pl.ds(col * 16, 16)], dinv, local_sem.at[1])
    dinv_copy.start()

    barrier = pltpu.get_barrier_semaphore()

    @pl.loop(1, 16)
    def _(o):
        pl.semaphore_signal(barrier, inc=1, device_id=((row + o) % 16, col), device_id_type=MESH)

    for d in (x_right, x_left, dev(z, yh, p, x2, yl), y_near):
        pl.semaphore_signal(barrier, inc=1, device_id=d, device_id_type=MESH)

    @pl.when(moves_near)
    def _():
        pl.semaphore_signal(barrier, inc=1, device_id=y_other, device_id_type=MESH)

    for s in range(HALVES):
        for b in range(rows // W):
            keep = mask[row * (rows // W) + b, col * HALVES + s].astype(F32)
            block = fac[b * W : (b + 1) * W, s * W : (s + 1) * W].astype(F32)
            masked[s, b * W : (b + 1) * W, :] = (block * keep).astype(BF)

    pl.semaphore_wait(barrier, jnp.where(moves_near, 20, 19))

    pending = []

    def remote(src, dst, send, recv, i, device):
        return pltpu.make_async_remote_copy(
            src_ref=src, dst_ref=dst, send_sem=send.at[i], recv_sem=recv.at[i],
            device_id=device, device_id_type=MESH,
        )

    halves = (slice(0, rows // 2), slice(rows // 2, rows))
    quarters = [[slice((r * 2 + h) * rows // 4, (r * 2 + h + 1) * rows // 4) for h in range(2)] for r in range(2)]

    gcopies = {}

    def start_gather(u, i, src, device, r):
        ref = x.at[u, p, src, halves[r]]
        c = remote(ref, ref, g_send, g_recv, u * GATHER + i, device)
        c.start()
        gcopies[u, i] = c
        pending.append(c)

    def got(u, i):
        gcopies[u, i].wait_recv()

    def to_hub(q, h):
        s, r = divmod(q, 2)
        j = (xi - z + 4) % 4 if h == 0 else (z - xi + 4) % 4
        device = dev(z, yh, p, z, yl) if h == 0 else dev(xi, yh, p, xi, yl)
        i = (q * 2 + h) * 4
        return pltpu.make_async_remote_copy(
            src_ref=masked.at[s, quarters[r][h]], dst_ref=hub.at[q, h, j],
            send_sem=h_send.at[q * 2 + h], recv_sem=h_recv.at[i + j],
            device_id=device, device_id_type=MESH,
        )

    def from_hub(q, h, j):
        s, r = divmod(q, 2)
        device = dev((z + j) % 4, yh, p, xi, yl) if h == 0 else dev(z, yh, p, (xi + j) % 4, yl)
        i = (q * 2 + h) * 4
        return pltpu.make_async_remote_copy(
            src_ref=hub.at[q, h, j], dst_ref=turned.at[s, quarters[r][h]],
            send_sem=f_send.at[i + j], recv_sem=t_recv.at[q * 2 + h],
            device_id=device, device_id_type=MESH,
        )

    def at_hub(q, h, j):
        s, r = divmod(q, 2)
        i = (q * 2 + h) * 4
        return pltpu.make_async_copy(masked.at[s, quarters[r][h]], hub.at[q, h, j], h_recv.at[i + j])

    def stay(q, h):
        s, r = divmod(q, 2)
        rows_of = quarters[r][h]
        return pltpu.make_async_copy(masked.at[s, rows_of], turned.at[s, rows_of], t_recv.at[q * 2 + h])

    def start_turn(q):
        for h in range(2):
            @pl.when(jnp.logical_not(on_diagonal))
            def _():
                to_hub(q, h).start()

            @pl.when(on_diagonal)
            def _():
                stay(q, h).start()

    def pass_hub(q):
        @pl.when(on_diagonal)
        def _():
            for j in (1, 3, 2):
                for h in range(2):
                    at_hub(q, h, j).wait()
                    from_hub(q, h, j).start()

        @pl.when(jnp.logical_not(on_diagonal))
        def _():
            for h in range(2):
                to_hub(q, h).wait_send()

    def end_hub():
        @pl.when(on_diagonal)
        def _():
            for q in range(4):
                for h in range(2):
                    for j in (1, 3, 2):
                        from_hub(q, h, j).wait_send()

    def near_copies(u, c, r):
        src, dst = turned.at[u // 2, halves[r]], x.at[u, p, z, halves[r]]
        recv = g_recv.at[u * GATHER + Y + r]
        away = pltpu.make_async_remote_copy(
            src_ref=src, dst_ref=dst, send_sem=y_send.at[(u * 2 + c) * 2 + r], recv_sem=recv,
            device_id=dev(z, c, p, xi, yh), device_id_type=MESH,
        )
        stays = jnp.logical_and(yh == c, yl == yh)
        return away, lambda: pltpu.make_async_copy(src, dst, recv), stays

    def end_near():
        for u in range(SLOTS):
            for c in range(2):
                for r in range(2):
                    @pl.when(yl == u % 2)
                    def _():
                        away, here, stays = near_copies(u, c, r)

                        @pl.when(jnp.logical_not(stays))
                        def _():
                            away.wait_send()

    def spread_near(q):
        s, r = divmod(q, 2)
        for h in range(2):
            stay(q, h).wait()
        for e in range(2):
            for c in range(2):
                @pl.when(yl == e)
                def _():
                    away, here, stays = near_copies(s * 2 + e, c, r)

                    @pl.when(jnp.logical_not(stays))
                    def _():
                        away.start()

                    @pl.when(stays)
                    def _():
                        here().start()

    def event1(u, r):
        near_copies(u, 0, r)[1]().wait()
        start_gather(u, ZR + r, z, z_right, r)
        start_gather(u, ZL + r, z, z_left, r)
        start_gather(u, SIB + r, z, sibling, r)

    def event2(u, r):
        if r == 0:
            got(u, ZR)
            start_gather(u, RR, zl, z_right, 0)
            start_gather(u, SIB + 2, zl, sibling, 0)
        else:
            got(u, ZL + 1)
            start_gather(u, RL, zr, z_left, 1)
            start_gather(u, SIB + 3, zr, sibling, 1)

    def event3(u):
        got(u, ZL)
        start_gather(u, SIB + 4, zr, sibling, 0)
        got(u, ZR + 1)
        start_gather(u, SIB + 5, zl, sibling, 1)
        got(u, RR)
        start_gather(u, SIB + 6, z2, sibling, 0)
        got(u, RL)
        start_gather(u, SIB + 7, z2, sibling, 1)

    def event4(u):
        for i in range(8):
            got(u, SIB + i)

    def product(t, first, second):
        u, m = divmod(t, PARTS)
        here = slice(m * slice_rows, (m + 1) * slice_rows)
        total = None
        for half in range(2):
            right = jnp.concatenate([x[u, half, first], x[u, half, second]], axis=1)
            term = jnp.dot(a[here, half * rows : (half + 1) * rows], right, preferred_element_type=F32)
            total = term if total is None else total + term
        return total

    rcopies = {}

    def start_reduce(t, i, src, dst, device):
        c = remote(src, dst, r_send, r_recv, t * REDUCE + i, device)
        c.start()
        rcopies[t, i] = c
        pending.append(c)

    def arrived(t, i):
        rcopies[t, i].wait_recv()

    top, low = slice(0, slice_rows // 2), slice(slice_rows // 2, slice_rows)

    def multiply(t):
        block = product(t, xr, x2)
        part[t, 0] = block[:, :W].astype(BF)
        part[t, 1] = block[:, W:].astype(BF)
        start_reduce(t, QR, part.at[t, 1, top], relay.at[t, 0], x_right)
        start_reduce(t, QL, part.at[t, 1, low], relay.at[t, 1], x_left)
        start_reduce(t, FR1, part.at[t, 0, low], fin.at[t, 0, low], x_right)
        block = product(t, xl, xi)
        part[t, 2] = block[:, :W].astype(BF)
        start_reduce(t, FL0, part.at[t, 2, top], fin.at[t, 1, top], x_left)
        own[t] = block[:, W:]

    def pass_on(t):
        arrived(t, QR)
        part[t, 0, top] = (part[t, 0, top].astype(F32) + relay[t, 0].astype(F32)).astype(BF)
        start_reduce(t, FR0, part.at[t, 0, top], fin.at[t, 0, top], x_right)
        arrived(t, QL)
        part[t, 2, low] = (part[t, 2, low].astype(F32) + relay[t, 1].astype(F32)).astype(BF)
        start_reduce(t, FL1, part.at[t, 2, low], fin.at[t, 1, low], x_left)

    def cross(t):
        return remote(ysend.at[t], yrecv.at[t], r_send, r_recv, t * REDUCE + YL, y_near)

    def finish(t):
        e = (t // PARTS) % 2
        for i in (FR0, FR1, FL0, FL1):
            arrived(t, i)

        @pl.when(yl == e)
        def _():
            own[t] = own[t] + fin[t, 0].astype(F32) + fin[t, 1].astype(F32)

        @pl.when(yl != e)
        def _():
            ysend[t] = (own[t] + fin[t, 0].astype(F32) + fin[t, 1].astype(F32)).astype(BF)
            cross(t).start()

    def put(t):
        u, m = divmod(t, PARTS)
        s, e = divmod(u, 2)
        here = slice(m * slice_rows, (m + 1) * slice_rows)

        @pl.when(yl == e)
        def _():
            cross(t).wait_recv()
            result = (own[t] + yrecv[t].astype(F32)).T
            off[s * W : (s + 1) * W, here] = (-result).astype(BF)
            high = result.astype(BF)
            rest = (result - high.astype(F32)).astype(BF)
            right = masked[s, here, :]
            term = jnp.dot(high, right, preferred_element_type=F32) + jnp.dot(
                rest, right, preferred_element_type=F32
            )
            dacc[s] += term

    start_turn(0)
    start_turn(1)
    pass_hub(0)
    start_turn(2)
    spread_near(0)
    pass_hub(1)
    spread_near(1)
    event1(1, 0)
    event1(0, 0)
    event1(0, 1)
    a_copy.wait()
    dinv_copy.wait()
    pass_hub(2)
    event2(0, 0)
    event1(1, 1)
    spread_near(2)
    start_turn(3)
    pass_hub(3)
    event2(0, 1)
    spread_near(3)
    event1(2, 0)
    event2(1, 0)
    event2(1, 1)
    event3(0)
    event4(0)
    multiply(2)
    event1(2, 1)
    multiply(1)
    event3(1)
    event2(2, 0)
    multiply(0)
    pass_on(2)
    event4(1)
    event2(2, 1)
    pass_on(1)
    multiply(3)
    event1(3, 1)
    multiply(5)
    event1(3, 0)
    finish(1)
    event3(2)
    pass_on(0)
    multiply(4)
    finish(2)
    pass_on(3)
    event4(2)
    multiply(6)
    event2(3, 0)
    event2(3, 1)
    finish(0)
    multiply(8)
    pass_on(5)
    finish(3)
    multiply(7)
    event3(3)
    pass_on(4)
    pass_on(6)
    event4(3)
    multiply(9)
    put(1)
    put(2)
    multiply(11)
    finish(6)
    finish(4)
    pass_on(9)
    finish(5)
    pass_on(7)
    multiply(10)
    put(3)
    put(6)
    pass_on(11)
    finish(7)
    finish(9)
    pass_on(8)
    put(4)
    pass_on(10)
    finish(11)
    put(5)
    finish(8)
    finish(10)
    put(0)
    put(9)
    put(7)
    put(11)
    put(8)
    put(10)

    for s in range(HALVES):
        dsend[s * 8 : (s + 1) * 8] = dacc[s].T.reshape(8, 16, W)

    def scatter_copy(o):
        to = (row + o) % 16
        return remote(dsend.at[to], drecv.at[o], d_send, d_recv, o, (to, col))

    def spread_copy(o):
        to = (row + o) % 16
        return remote(dsum, dall.at[row], d_send, d_recv, 16 + o, (to, col))

    @pl.loop(1, 16)
    def _(o):
        scatter_copy(o).start()

    @pl.loop(1, 16)
    def _(o):
        scatter_copy(o).wait_recv()

    total = dsend[row] + dinv[row]
    for o in range(1, 16):
        total = total + drecv[o]
    dsum[...] = total

    @pl.loop(1, 16)
    def _(o):
        spread_copy(o).start()

    diag[row] = total

    @pl.loop(1, 16)
    def _(o):
        spread_copy(o).wait_recv()
        since = (row + 16 - o) % 16
        diag[since] = dall[since]

    @pl.loop(1, 16)
    def _(o):
        scatter_copy(o).wait_send()
        spread_copy(o).wait_send()

    for c in pending:
        c.wait_send()
    end_near()
    for t in range(STEPS):
        @pl.when(yl != (t // PARTS) % 2)
        def _():
            cross(t).wait_send()

    end_hub()


def per_device(inverse_tiles, factor, block_mask, diag_inverse):
    rows, depth = inverse_tiles.shape
    cols = factor.shape[1]
    part_rows = rows // PARTS
    vmem = pl.BlockSpec(memory_space=pltpu.VMEM)
    anywhere = pl.BlockSpec(memory_space=pl.ANY)
    off, diag = pl.pallas_call(
        kernel,
        out_shape=(
            jax.ShapeDtypeStruct((cols, rows), BF),
            jax.ShapeDtypeStruct((16, 16, W), F32),
        ),
        in_specs=[vmem, anywhere, pl.BlockSpec(memory_space=pltpu.SMEM), anywhere],
        out_specs=(vmem, vmem),
        scratch_shapes=[
            pltpu.VMEM((rows, depth), BF),
            pltpu.VMEM((16, 16, W), F32),
            pltpu.VMEM((HALVES, rows, W), BF),
            pltpu.VMEM((SLOTS, 2, 4, rows, W), BF),
            pltpu.VMEM((HALVES * 2, 2, 4, rows // 4, W), BF),
            pltpu.VMEM((HALVES, rows, W), BF),
            pltpu.VMEM((STEPS, 3, part_rows, W), BF),
            pltpu.VMEM((STEPS, part_rows, W), F32),
            pltpu.VMEM((STEPS, 2, part_rows // 2, W), BF),
            pltpu.VMEM((STEPS, 2, part_rows, W), BF),
            pltpu.VMEM((STEPS, part_rows, W), BF),
            pltpu.VMEM((STEPS, part_rows, W), BF),
            pltpu.VMEM((HALVES, W, W), F32),
            pltpu.VMEM((16, 16, W), F32),
            pltpu.VMEM((16, 16, W), F32),
            pltpu.VMEM((16, W), F32),
            pltpu.VMEM((16, 16, W), F32),
            pltpu.SemaphoreType.DMA((2,)),
            pltpu.SemaphoreType.DMA((SLOTS * GATHER,)),
            pltpu.SemaphoreType.DMA((SLOTS * GATHER,)),
            pltpu.SemaphoreType.DMA((SLOTS * 4,)),
            pltpu.SemaphoreType.DMA((8,)),
            pltpu.SemaphoreType.DMA((32,)),
            pltpu.SemaphoreType.DMA((32,)),
            pltpu.SemaphoreType.DMA((8,)),
            pltpu.SemaphoreType.DMA((STEPS * REDUCE,)),
            pltpu.SemaphoreType.DMA((STEPS * REDUCE,)),
            pltpu.SemaphoreType.DMA((32,)),
            pltpu.SemaphoreType.DMA((32,)),
        ],
        compiler_params=pltpu.CompilerParams(
            collective_id=0, has_side_effects=True, vmem_limit_bytes=58 * 1024 * 1024
        ),
    )(factor, inverse_tiles, block_mask, diag_inverse.reshape(8 * 16, 16, W))
    return off, diag.reshape(2, W, W)


def solution(mesh):
    return jax.shard_map(
        per_device,
        mesh=mesh,
        in_specs=(P("row", "col"), P("row", "col"), P(), P()),
        out_specs=(P("col", "row"), P("col", None, None)),
        check_vma=False,
    )
```

time: 194 us -> 155 us (0.80)
  Pallas kernels: 187 us -> 148 us
    pallas_call x1, Pallas kernels: 187 us -> 148 us  [per_device(): pl.pallas_call(kernel, out_shape=(jax.ShapeDtypeStruct((cols, rows), BF),...]
where the time goes in v3:
time: 155 us; the launch traced here: 153 us
  Pallas kernels  148 us (95%)
  local copies, waits for them, and re-layouts  5.09 us (3%)
    pallas_call x1, Pallas kernels, per_device(): pl.pallas_call(kernel, out_shape=(jax.ShapeDtypeStruct((cols, rows), BF),...  148 us
    unnamed x3, local copies, waits for them, and re-layouts  5.09 us

profile of v3, /device:TPU:1, one launch (start us, length us, event | category | flops | bytes accessed | tf_op | source)
XLA Modules:
  0.0 153.3 jit_solution(9749028229448493459)
XLA Ops:
  0.6 1.5 copy.6.mask
  2.1 147.6 %shard_map.59 = (bf16[256,1536]{1,0:T(8,128)(2,1)}, f32[16,16,128]{2,1,0:T(8,128)}) custom-call(bf16[1536,256]{1,0:T(8,128)(2,1)} %fac.1, bf16[1536,3072]{1,0:T(8,128)(2,1)} %a_hbm.1, s32[192,16]{1,0:T(8,128)} %copy.6.mask, f32[128,16,128]{2,1,0:T(8,128)} %bitcast.2), custom_call_target="tpu_custom_call" | custom-call | tf_op jit(solution)/shard_map/pallas_call | solution.py:454
  149.6 2.1 %copy.9 = bf16[256,1536]{1,0:T(8,128)(2,1)} copy(bf16[256,1536]{1,0:T(8,128)(2,1)} %get-tuple-element.8) | data formatting | bytes 1572864
  151.7 1.6 %copy.10 = f32[2,128,128]{2,1,0:T(8,128)} copy(f32[2,128,128]{2,1,0:T(8,128)} %bitcast.3) | data formatting | bytes 262144

commit v4 on v3

--- a/solution.py
+++ b/solution.py
@@ -14,10 +14,12 @@
 PARTS = 3
 STEPS = SLOTS * PARTS
 
-Y, ZR, ZL = 0, 2, 4
-RR, RL = 6, 7
-SIB = 8
-GATHER = 16
+PIECES = (4, 2)
+QUEUE = [(s, r) for s in range(HALVES) for r in range(PIECES[s])]
+
+Y, ZR, ZL, ON = 0, 4, 8, 12
+SIB = 16
+GATHER = 28
 QR, QL, FR0, FR1, FL0, FL1, YL = range(7)
 REDUCE = 7
 
@@ -82,12 +84,23 @@
         )
 
     halves = (slice(0, rows // 2), slice(rows // 2, rows))
-    quarters = [[slice((r * 2 + h) * rows // 4, (r * 2 + h + 1) * rows // 4) for h in range(2)] for r in range(2)]
+
+    def piece(s, r):
+        size = rows // PIECES[s]
+        return slice(r * size, (r + 1) * size)
+
+    def piece_half(s, r, h):
+        size = rows // PIECES[s] // 2
+        return slice((r * 2 + h) * size, (r * 2 + h + 1) * size)
+
+    def in_hub(s, r):
+        size = rows // PIECES[s] // 2
+        return slice(r * size, (r + 1) * size)
 
     gcopies = {}
 
-    def start_gather(u, i, src, device, r):
-        ref = x.at[u, p, src, halves[r]]
+    def start_gather(u, i, src, device, lines):
+        ref = x.at[u, p, src, lines]
         c = remote(ref, ref, g_send, g_recv, u * GATHER + i, device)
         c.start()
         gcopies[u, i] = c
@@ -97,34 +110,34 @@
         gcopies[u, i].wait_recv()
 
     def to_hub(q, h):
-        s, r = divmod(q, 2)
+        s, r = QUEUE[q]
         j = (xi - z + 4) % 4 if h == 0 else (z - xi + 4) % 4
         device = dev(z, yh, p, z, yl) if h == 0 else dev(xi, yh, p, xi, yl)
         i = (q * 2 + h) * 4
         return pltpu.make_async_remote_copy(
-            src_ref=masked.at[s, quarters[r][h]], dst_ref=hub.at[q, h, j],
+            src_ref=masked.at[s, piece_half(s, r, h)], dst_ref=hub.at[s, h, j, in_hub(s, r)],
             send_sem=h_send.at[q * 2 + h], recv_sem=h_recv.at[i + j],
             device_id=device, device_id_type=MESH,
         )
 
     def from_hub(q, h, j):
-        s, r = divmod(q, 2)
+        s, r = QUEUE[q]
         device = dev((z + j) % 4, yh, p, xi, yl) if h == 0 else dev(z, yh, p, (xi + j) % 4, yl)
         i = (q * 2 + h) * 4
         return pltpu.make_async_remote_copy(
-            src_ref=hub.at[q, h, j], dst_ref=turned.at[s, quarters[r][h]],
+            src_ref=hub.at[s, h, j, in_hub(s, r)], dst_ref=turned.at[s, piece_half(s, r, h)],
             send_sem=f_send.at[i + j], recv_sem=t_recv.at[q * 2 + h],
             device_id=device, device_id_type=MESH,
         )
 
     def at_hub(q, h, j):
-        s, r = divmod(q, 2)
+        s, r = QUEUE[q]
         i = (q * 2 + h) * 4
-        return pltpu.make_async_copy(masked.at[s, quarters[r][h]], hub.at[q, h, j], h_recv.at[i + j])
+        return pltpu.make_async_copy(masked.at[s, piece_half(s, r, h)], hub.at[s, h, j, in_hub(s, r)], h_recv.at[i + j])
 
     def stay(q, h):
-        s, r = divmod(q, 2)
-        rows_of = quarters[r][h]
+        s, r = QUEUE[q]
+        rows_of = piece_half(s, r, h)
         return pltpu.make_async_copy(masked.at[s, rows_of], turned.at[s, rows_of], t_recv.at[q * 2 + h])
 
     def start_turn(q):
@@ -153,16 +166,17 @@
     def end_hub():
         @pl.when(on_diagonal)
         def _():
-            for q in range(4):
+            for q in range(len(QUEUE)):
                 for h in range(2):
                     for j in (1, 3, 2):
                         from_hub(q, h, j).wait_send()
 
     def near_copies(u, c, r):
-        src, dst = turned.at[u // 2, halves[r]], x.at[u, p, z, halves[r]]
+        lines = piece(u // 2, r)
+        src, dst = turned.at[u // 2, lines], x.at[u, p, z, lines]
         recv = g_recv.at[u * GATHER + Y + r]
         away = pltpu.make_async_remote_copy(
-            src_ref=src, dst_ref=dst, send_sem=y_send.at[(u * 2 + c) * 2 + r], recv_sem=recv,
+            src_ref=src, dst_ref=dst, send_sem=y_send.at[(u * 2 + c) * 4 + r], recv_sem=recv,
             device_id=dev(z, c, p, xi, yh), device_id_type=MESH,
         )
         stays = jnp.logical_and(yh == c, yl == yh)
@@ -171,7 +185,7 @@
     def end_near():
         for u in range(SLOTS):
             for c in range(2):
-                for r in range(2):
+                for r in range(PIECES[u // 2]):
                     @pl.when(yl == u % 2)
                     def _():
                         away, here, stays = near_copies(u, c, r)
@@ -181,7 +195,7 @@
                             away.wait_send()
 
     def spread_near(q):
-        s, r = divmod(q, 2)
+        s, r = QUEUE[q]
         for h in range(2):
             stay(q, h).wait()
         for e in range(2):
@@ -200,32 +214,40 @@
 
     def event1(u, r):
         near_copies(u, 0, r)[1]().wait()
-        start_gather(u, ZR + r, z, z_right, r)
-        start_gather(u, ZL + r, z, z_left, r)
-        start_gather(u, SIB + r, z, sibling, r)
+        lines = piece(u // 2, r)
+        start_gather(u, ZR + r, z, z_right, lines)
+        start_gather(u, ZL + r, z, z_left, lines)
+        start_gather(u, SIB + r, z, sibling, lines)
 
     def event2(u, r):
-        if r == 0:
-            got(u, ZR)
-            start_gather(u, RR, zl, z_right, 0)
-            start_gather(u, SIB + 2, zl, sibling, 0)
+        n = PIECES[u // 2]
+        lines = piece(u // 2, r)
+        if r < n // 2:
+            got(u, ZR + r)
+            start_gather(u, ON + r, zl, z_right, lines)
+            start_gather(u, SIB + n + r, zl, sibling, lines)
         else:
-            got(u, ZL + 1)
-            start_gather(u, RL, zr, z_left, 1)
-            start_gather(u, SIB + 3, zr, sibling, 1)
+            got(u, ZL + r)
+            start_gather(u, ON + r, zr, z_left, lines)
+            start_gather(u, SIB + n + r, zr, sibling, lines)
 
     def event3(u):
-        got(u, ZL)
-        start_gather(u, SIB + 4, zr, sibling, 0)
-        got(u, ZR + 1)
-        start_gather(u, SIB + 5, zl, sibling, 1)
-        got(u, RR)
-        start_gather(u, SIB + 6, z2, sibling, 0)
-        got(u, RL)
-        start_gather(u, SIB + 7, z2, sibling, 1)
+        n = PIECES[u // 2]
+        for r in range(n // 2):
+            got(u, ZL + r)
+        start_gather(u, SIB + 2 * n, zr, sibling, halves[0])
+        for r in range(n // 2, n):
+            got(u, ZR + r)
+        start_gather(u, SIB + 2 * n + 1, zl, sibling, halves[1])
+        for r in range(n // 2):
+            got(u, ON + r)
+        start_gather(u, SIB + 2 * n + 2, z2, sibling, halves[0])
+        for r in range(n // 2, n):
+            got(u, ON + r)
+        start_gather(u, SIB + 2 * n + 3, z2, sibling, halves[1])
 
     def event4(u):
-        for i in range(8):
+        for i in range(2 * PIECES[u // 2] + 4):
             got(u, SIB + i)
 
     def product(t, first, second):
@@ -308,87 +330,101 @@
 
     start_turn(0)
     start_turn(1)
+    start_turn(2)
     pass_hub(0)
-    start_turn(2)
+    pass_hub(1)
+    pass_hub(2)
     spread_near(0)
-    pass_hub(1)
+    start_turn(3)
+    a_copy.wait()
+    dinv_copy.wait()
+    pass_hub(3)
     spread_near(1)
     event1(1, 0)
+    spread_near(2)
     event1(0, 0)
+    spread_near(3)
     event1(0, 1)
-    a_copy.wait()
-    dinv_copy.wait()
-    pass_hub(2)
+    start_turn(4)
+    pass_hub(4)
+    start_turn(5)
+    event1(0, 2)
+    event1(0, 3)
+    pass_hub(5)
     event2(0, 0)
+    event2(0, 1)
+    spread_near(4)
+    event2(0, 2)
+    event2(0, 3)
+    spread_near(5)
+    event1(1, 2)
     event1(1, 1)
-    spread_near(2)
-    start_turn(3)
-    pass_hub(3)
-    event2(0, 1)
-    spread_near(3)
+    event3(0)
+    event2(1, 0)
+    event1(1, 3)
+    event2(1, 2)
+    event4(0)
+    multiply(1)
+    event2(1, 1)
+    event2(1, 3)
+    multiply(0)
+    event1(2, 1)
+    pass_on(1)
+    event3(1)
     event1(2, 0)
-    event2(1, 0)
-    event2(1, 1)
-    event3(0)
-    event4(0)
     multiply(2)
-    event1(2, 1)
-    multiply(1)
-    event3(1)
+    event2(2, 1)
+    pass_on(0)
+    event4(1)
+    multiply(4)
     event2(2, 0)
-    multiply(0)
     pass_on(2)
-    event4(1)
-    event2(2, 1)
-    pass_on(1)
     multiply(3)
+    event1(3, 0)
+    multiply(5)
+    finish(1)
+    pass_on(4)
     event1(3, 1)
-    multiply(5)
-    event1(3, 0)
-    finish(1)
     event3(2)
-    pass_on(0)
-    multiply(4)
-    finish(2)
     pass_on(3)
     event4(2)
     multiply(6)
+    event2(3, 1)
     event2(3, 0)
-    event2(3, 1)
+    multiply(7)
+    pass_on(5)
     finish(0)
+    finish(3)
     multiply(8)
-    pass_on(5)
-    finish(3)
-    multiply(7)
+    pass_on(6)
     event3(3)
-    pass_on(4)
-    pass_on(6)
+    finish(4)
+    put(3)
+    pass_on(7)
     event4(3)
     multiply(9)
+    put(0)
+    multiply(11)
+    finish(7)
+    finish(5)
+    finish(6)
+    pass_on(9)
+    multiply(10)
     put(1)
-    put(2)
-    multiply(11)
-    finish(6)
-    finish(4)
-    pass_on(9)
-    finish(5)
-    pass_on(7)
-    multiply(10)
-    put(3)
-    put(6)
+    put(4)
     pass_on(11)
-    finish(7)
+    finish(2)
     finish(9)
     pass_on(8)
-    put(4)
+    put(7)
     pass_on(10)
     finish(11)
-    put(5)
+    put(6)
     finish(8)
     finish(10)
-    put(0)
+    put(2)
+    put(5)
     put(9)
-    put(7)
     put(11)
     put(8)
     put(10)
@@ -464,7 +500,7 @@
             pltpu.VMEM((16, 16, W), F32),
             pltpu.VMEM((HALVES, rows, W), BF),
             pltpu.VMEM((SLOTS, 2, 4, rows, W), BF),
-            pltpu.VMEM((HALVES * 2, 2, 4, rows // 4, W), BF),
+            pltpu.VMEM((HALVES, 2, 4, rows // 2, W), BF),
             pltpu.VMEM((HALVES, rows, W), BF),
             pltpu.VMEM((STEPS, 3, part_rows, W), BF),
             pltpu.VMEM((STEPS, part_rows, W), F32),
@@ -480,11 +516,11 @@
             pltpu.SemaphoreType.DMA((2,)),
             pltpu.SemaphoreType.DMA((SLOTS * GATHER,)),
             pltpu.SemaphoreType.DMA((SLOTS * GATHER,)),
-            pltpu.SemaphoreType.DMA((SLOTS * 4,)),
-            pltpu.SemaphoreType.DMA((8,)),
-            pltpu.SemaphoreType.DMA((32,)),
-            pltpu.SemaphoreType.DMA((32,)),
-            pltpu.SemaphoreType.DMA((8,)),
+            pltpu.SemaphoreType.DMA((SLOTS * 8,)),
+            pltpu.SemaphoreType.DMA((len(QUEUE) * 2,)),
+            pltpu.SemaphoreType.DMA((len(QUEUE) * 8,)),
+            pltpu.SemaphoreType.DMA((len(QUEUE) * 8,)),
+            pltpu.SemaphoreType.DMA((len(QUEUE) * 2,)),
             pltpu.SemaphoreType.DMA((STEPS * REDUCE,)),
             pltpu.SemaphoreType.DMA((STEPS * REDUCE,)),
             pltpu.SemaphoreType.DMA((32,)),

time: 155 us -> 149 us (0.961)
  Pallas kernels: 148 us -> 143 us
    pallas_call x1, Pallas kernels: 148 us -> 143 us  [per_device(): pl.pallas_call(kernel, out_shape=(jax.ShapeDtypeStruct((cols, rows), BF),...]
where the time goes in v4:
time: 149 us
  Pallas kernels  143 us (96%)
  local copies, waits for them, and re-layouts  5.09 us (3%)
    pallas_call x1, Pallas kernels, per_device(): pl.pallas_call(kernel, out_shape=(jax.ShapeDtypeStruct((cols, rows), BF),...  143 us
    unnamed x3, local copies, waits for them, and re-layouts  5.09 us

profile of v4, /device:TPU:1, one launch (start us, length us, event | category | flops | bytes accessed | tf_op | source)
XLA Modules:
  0.0 148.8 jit_solution(299514981550756975)
XLA Ops:
  0.6 1.5 copy.6.mask
  2.1 143.0 %shard_map.59 = (bf16[256,1536]{1,0:T(8,128)(2,1)}, f32[16,16,128]{2,1,0:T(8,128)}) custom-call(bf16[1536,256]{1,0:T(8,128)(2,1)} %fac.1, bf16[1536,3072]{1,0:T(8,128)(2,1)} %a_hbm.1, s32[192,16]{1,0:T(8,128)} %copy.6.mask, f32[128,16,128]{2,1,0:T(8,128)} %bitcast.2), custom_call_target="tpu_custom_call" | custom-call | tf_op jit(solution)/shard_map/pallas_call | solution.py:490
  145.1 2.1 %copy.9 = bf16[256,1536]{1,0:T(8,128)(2,1)} copy(bf16[256,1536]{1,0:T(8,128)(2,1)} %get-tuple-element.8) | data formatting | bytes 1572864
  147.2 1.6 %copy.10 = f32[2,128,128]{2,1,0:T(8,128)} copy(f32[2,128,128]{2,1,0:T(8,128)} %bitcast.3) | data formatting | bytes 262144

commit v5 on v4

--- a/solution.py
+++ b/solution.py
@@ -12,6 +12,7 @@
 HALVES = 2
 SLOTS = 4
 PARTS = 3
+SHARES = ((4, 4, 4), (4, 4, 4), (4, 4, 4), (5, 5, 2))
 STEPS = SLOTS * PARTS
 
 PIECES = (4, 2)
@@ -19,18 +20,30 @@
 
 Y, ZR, ZL, ON = 0, 4, 8, 12
 SIB = 16
-GATHER = 28
-QR, QL, FR0, FR1, FL0, FL1, YL = range(7)
-REDUCE = 7
+SENDS = 24
+ARRIVALS = (0, 28, 56, 72)
+QR, QL, FR0, FR1, FL0, FL1 = range(6)
+REDUCE = 6
+TURNS = 6
 
 
 def kernel(
     fac, a_hbm, mask, dinv_hbm, off, diag,
     a, dinv, masked, x, hub, turned, part, own, relay, fin, ysend, yrecv, dacc, dsend, drecv, dsum, dall,
-    local_sem, g_send, g_recv, y_send, h_send, h_recv, f_send, t_recv, r_send, r_recv, d_send, d_recv,
+    local_sem, g_send, g_recv, y_send, h_recv, f_send, t_recv, r_send, r_recv, c_send, c_recv, d_send, d_recv,
 ):
     rows = fac.shape[0]
-    slice_rows = rows // PARTS
+    unit = rows // 12
+
+    def step_rows(t):
+        u, m = divmod(t, PARTS)
+        first = sum(SHARES[u][:m])
+        return slice(first * unit, (first + SHARES[u][m]) * unit)
+
+    def step_size(t):
+        u, m = divmod(t, PARTS)
+        return SHARES[u][m] * unit
+
     row, col = lax.axis_index("row"), lax.axis_index("col")
     z, yh, p = row // 4, (row // 2) % 2, row % 2
     xi, yl = col // 2, col % 2
@@ -75,13 +88,18 @@
 
     pl.semaphore_wait(barrier, jnp.where(moves_near, 20, 19))
 
-    pending = []
-
-    def remote(src, dst, send, recv, i, device):
+    active = {}
+
+    def remote(src, dst, send, recv, device):
         return pltpu.make_async_remote_copy(
-            src_ref=src, dst_ref=dst, send_sem=send.at[i], recv_sem=recv.at[i],
-            device_id=device, device_id_type=MESH,
+            src_ref=src, dst_ref=dst, send_sem=send, recv_sem=recv, device_id=device, device_id_type=MESH,
         )
+
+    def start(copy, kind, i):
+        if (kind, i) in active:
+            active[kind, i].wait_send()
+        copy.start()
+        active[kind, i] = copy
 
     halves = (slice(0, rows // 2), slice(rows // 2, rows))
 
@@ -100,11 +118,13 @@
     gcopies = {}
 
     def start_gather(u, i, src, device, lines):
+        n = PIECES[u // 2]
+        i_here = 3 * n + i - SIB if i >= SIB else (i // 4 - 1) * n + i % 4
         ref = x.at[u, p, src, lines]
-        c = remote(ref, ref, g_send, g_recv, u * GATHER + i, device)
-        c.start()
+        i_send = u % 2 * SENDS + i_here
+        c = remote(ref, ref, g_send.at[i_send], g_recv.at[ARRIVALS[u] + n + i_here], device)
+        start(c, "gather", i_send)
         gcopies[u, i] = c
-        pending.append(c)
 
     def got(u, i):
         gcopies[u, i].wait_recv()
@@ -113,17 +133,17 @@
         s, r = QUEUE[q]
         j = (xi - z + 4) % 4 if h == 0 else (z - xi + 4) % 4
         device = dev(z, yh, p, z, yl) if h == 0 else dev(xi, yh, p, xi, yl)
-        i = (q * 2 + h) * 4
+        i = (q * 2 + h) * 3 - 1
         return pltpu.make_async_remote_copy(
             src_ref=masked.at[s, piece_half(s, r, h)], dst_ref=hub.at[s, h, j, in_hub(s, r)],
-            send_sem=h_send.at[q * 2 + h], recv_sem=h_recv.at[i + j],
+            send_sem=f_send.at[i + 1], recv_sem=h_recv.at[i + j],
             device_id=device, device_id_type=MESH,
         )
 
     def from_hub(q, h, j):
         s, r = QUEUE[q]
         device = dev((z + j) % 4, yh, p, xi, yl) if h == 0 else dev(z, yh, p, (xi + j) % 4, yl)
-        i = (q * 2 + h) * 4
+        i = (q * 2 + h) * 3 - 1
         return pltpu.make_async_remote_copy(
             src_ref=hub.at[s, h, j, in_hub(s, r)], dst_ref=turned.at[s, piece_half(s, r, h)],
             send_sem=f_send.at[i + j], recv_sem=t_recv.at[q * 2 + h],
@@ -132,7 +152,7 @@
 
     def at_hub(q, h, j):
         s, r = QUEUE[q]
-        i = (q * 2 + h) * 4
+        i = (q * 2 + h) * 3 - 1
         return pltpu.make_async_copy(masked.at[s, piece_half(s, r, h)], hub.at[s, h, j, in_hub(s, r)], h_recv.at[i + j])
 
     def stay(q, h):
@@ -174,9 +194,9 @@
     def near_copies(u, c, r):
         lines = piece(u // 2, r)
         src, dst = turned.at[u // 2, lines], x.at[u, p, z, lines]
-        recv = g_recv.at[u * GATHER + Y + r]
+        recv = g_recv.at[ARRIVALS[u] + r]
         away = pltpu.make_async_remote_copy(
-            src_ref=src, dst_ref=dst, send_sem=y_send.at[(u * 2 + c) * 4 + r], recv_sem=recv,
+            src_ref=src, dst_ref=dst, send_sem=y_send.at[u // 2 * 8 + c * PIECES[u // 2] + r], recv_sem=recv,
             device_id=dev(z, c, p, xi, yh), device_id_type=MESH,
         )
         stays = jnp.logical_and(yh == c, yl == yh)
@@ -252,7 +272,7 @@
 
     def product(t, first, second):
         u, m = divmod(t, PARTS)
-        here = slice(m * slice_rows, (m + 1) * slice_rows)
+        here = step_rows(t)
         total = None
         for half in range(2):
             right = jnp.concatenate([x[u, half, first], x[u, half, second]], axis=1)
@@ -263,62 +283,68 @@
     rcopies = {}
 
     def start_reduce(t, i, src, dst, device):
-        c = remote(src, dst, r_send, r_recv, t * REDUCE + i, device)
-        c.start()
+        i_send = t % TURNS * REDUCE + i
+        c = remote(src, dst, r_send.at[i_send], r_recv.at[t * REDUCE + i], device)
+        start(c, "reduce", i_send)
         rcopies[t, i] = c
-        pending.append(c)
 
     def arrived(t, i):
         rcopies[t, i].wait_recv()
 
-    top, low = slice(0, slice_rows // 2), slice(slice_rows // 2, slice_rows)
-
     def multiply(t):
+        n = step_size(t)
+        top, low, full = slice(0, n // 2), slice(n // 2, n), slice(0, n)
         block = product(t, xr, x2)
-        part[t, 0] = block[:, :W].astype(BF)
-        part[t, 1] = block[:, W:].astype(BF)
-        start_reduce(t, QR, part.at[t, 1, top], relay.at[t, 0], x_right)
-        start_reduce(t, QL, part.at[t, 1, low], relay.at[t, 1], x_left)
+        part[t, 0, full] = block[:, :W].astype(BF)
+        part[t, 1, full] = block[:, W:].astype(BF)
+        start_reduce(t, QR, part.at[t, 1, top], relay.at[t, 0, top], x_right)
+        start_reduce(t, QL, part.at[t, 1, low], relay.at[t, 1, top], x_left)
         start_reduce(t, FR1, part.at[t, 0, low], fin.at[t, 0, low], x_right)
         block = product(t, xl, xi)
-        part[t, 2] = block[:, :W].astype(BF)
+        part[t, 2, full] = block[:, :W].astype(BF)
         start_reduce(t, FL0, part.at[t, 2, top], fin.at[t, 1, top], x_left)
-        own[t] = block[:, W:]
+        own[t, full] = block[:, W:]
 
     def pass_on(t):
+        n = step_size(t)
+        top, low = slice(0, n // 2), slice(n // 2, n)
         arrived(t, QR)
-        part[t, 0, top] = (part[t, 0, top].astype(F32) + relay[t, 0].astype(F32)).astype(BF)
+        part[t, 0, top] = (part[t, 0, top].astype(F32) + relay[t, 0, top].astype(F32)).astype(BF)
         start_reduce(t, FR0, part.at[t, 0, top], fin.at[t, 0, top], x_right)
         arrived(t, QL)
-        part[t, 2, low] = (part[t, 2, low].astype(F32) + relay[t, 1].astype(F32)).astype(BF)
+        part[t, 2, low] = (part[t, 2, low].astype(F32) + relay[t, 1, top].astype(F32)).astype(BF)
         start_reduce(t, FL1, part.at[t, 2, low], fin.at[t, 1, low], x_left)
 
     def cross(t):
-        return remote(ysend.at[t], yrecv.at[t], r_send, r_recv, t * REDUCE + YL, y_near)
+        full = slice(0, step_size(t))
+        i = t // 6 * 3 + t % 3
+        return remote(ysend.at[t, full], yrecv.at[t, full], c_send.at[i], c_recv.at[i], y_near)
 
     def finish(t):
         e = (t // PARTS) % 2
+        full = slice(0, step_size(t))
         for i in (FR0, FR1, FL0, FL1):
             arrived(t, i)
 
         @pl.when(yl == e)
         def _():
-            own[t] = own[t] + fin[t, 0].astype(F32) + fin[t, 1].astype(F32)
+            own[t, full] = own[t, full] + fin[t, 0, full].astype(F32) + fin[t, 1, full].astype(F32)
 
         @pl.when(yl != e)
         def _():
-            ysend[t] = (own[t] + fin[t, 0].astype(F32) + fin[t, 1].astype(F32)).astype(BF)
+            total = own[t, full] + fin[t, 0, full].astype(F32) + fin[t, 1, full].astype(F32)
+            ysend[t, full] = total.astype(BF)
             cross(t).start()
 
     def put(t):
         u, m = divmod(t, PARTS)
         s, e = divmod(u, 2)
-        here = slice(m * slice_rows, (m + 1) * slice_rows)
+        here, full = step_rows(t), slice(0, step_size(t))
 
         @pl.when(yl == e)
         def _():
             cross(t).wait_recv()
-            result = (own[t] + yrecv[t].astype(F32)).T
+            result = (own[t, full] + yrecv[t, full].astype(F32)).T
             off[s * W : (s + 1) * W, here] = (-result).astype(BF)
             high = result.astype(BF)
             rest = (result - high.astype(F32)).astype(BF)
@@ -434,19 +460,29 @@
 
     def scatter_copy(o):
         to = (row + o) % 16
-        return remote(dsend.at[to], drecv.at[o], d_send, d_recv, o, (to, col))
+        return remote(dsend.at[to], drecv.at[o], d_send.at[o - 1], d_recv.at[o - 1], (to, col))
 
     def spread_copy(o):
         to = (row + o) % 16
-        return remote(dsum, dall.at[row], d_send, d_recv, 16 + o, (to, col))
+        return remote(dsum, dall.at[row], d_send.at[o - 1], d_recv.at[o + 14], (to, col))
 
     @pl.loop(1, 16)
     def _(o):
         scatter_copy(o).start()
 
+    for c in active.values():
+        c.wait_send()
+    end_near()
+    for t in range(STEPS):
+        @pl.when(yl != (t // PARTS) % 2)
+        def _():
+            cross(t).wait_send()
+
+    end_hub()
+
     @pl.loop(1, 16)
     def _(o):
-        scatter_copy(o).wait_recv()
+        scatter_copy(o).wait()
 
     total = dsend[row] + dinv[row]
     for o in range(1, 16):
@@ -467,24 +503,13 @@
 
     @pl.loop(1, 16)
     def _(o):
-        scatter_copy(o).wait_send()
         spread_copy(o).wait_send()
-
-    for c in pending:
-        c.wait_send()
-    end_near()
-    for t in range(STEPS):
-        @pl.when(yl != (t // PARTS) % 2)
-        def _():
-            cross(t).wait_send()
-
-    end_hub()
 
 
 def per_device(inverse_tiles, factor, block_mask, diag_inverse):
     rows, depth = inverse_tiles.shape
     cols = factor.shape[1]
-    part_rows = rows // PARTS
+    part_rows = rows // 12 * max(max(shares) for shares in SHARES)
     vmem = pl.BlockSpec(memory_space=pltpu.VMEM)
     anywhere = pl.BlockSpec(memory_space=pl.ANY)
     off, diag = pl.pallas_call(
@@ -514,17 +539,18 @@
             pltpu.VMEM((16, W), F32),
             pltpu.VMEM((16, 16, W), F32),
             pltpu.SemaphoreType.DMA((2,)),
-            pltpu.SemaphoreType.DMA((SLOTS * GATHER,)),
-            pltpu.SemaphoreType.DMA((SLOTS * GATHER,)),
-            pltpu.SemaphoreType.DMA((SLOTS * 8,)),
+            pltpu.SemaphoreType.DMA((2 * SENDS,)),
+            pltpu.SemaphoreType.DMA((88,)),
+            pltpu.SemaphoreType.DMA((12,)),
+            pltpu.SemaphoreType.DMA((len(QUEUE) * 6,)),
+            pltpu.SemaphoreType.DMA((len(QUEUE) * 6,)),
             pltpu.SemaphoreType.DMA((len(QUEUE) * 2,)),
-            pltpu.SemaphoreType.DMA((len(QUEUE) * 8,)),
-            pltpu.SemaphoreType.DMA((len(QUEUE) * 8,)),
-            pltpu.SemaphoreType.DMA((len(QUEUE) * 2,)),
+            pltpu.SemaphoreType.DMA((TURNS * REDUCE,)),
             pltpu.SemaphoreType.DMA((STEPS * REDUCE,)),
-            pltpu.SemaphoreType.DMA((STEPS * REDUCE,)),
-            pltpu.SemaphoreType.DMA((32,)),
-            pltpu.SemaphoreType.DMA((32,)),
+            pltpu.SemaphoreType.DMA((6,)),
+            pltpu.SemaphoreType.DMA((6,)),
+            pltpu.SemaphoreType.DMA((15,)),
+            pltpu.SemaphoreType.DMA((30,)),
         ],
         compiler_params=pltpu.CompilerParams(
             collective_id=0, has_side_effects=True, vmem_limit_bytes=58 * 1024 * 1024

time: 149 us -> 146 us (0.980)
  Pallas kernels: 143 us -> 140 us
    pallas_call x1, Pallas kernels: 143 us -> 140 us  [per_device(): pl.pallas_call(kernel, out_shape=(jax.ShapeDtypeStruct((cols, rows), BF),...]
where the time goes in v5:
time: 146 us
  Pallas kernels  140 us (96%)
  local copies, waits for them, and re-layouts  5.09 us (3%)
    pallas_call x1, Pallas kernels, per_device(): pl.pallas_call(kernel, out_shape=(jax.ShapeDtypeStruct((cols, rows), BF),...  140 us
    unnamed x3, local copies, waits for them, and re-layouts  5.09 us

profile of v5, /device:TPU:1, one launch (start us, length us, event | category | flops | bytes accessed | tf_op | source)
XLA Modules:
  0.0 145.9 jit_solution(5994357386510283266)
XLA Ops:
  0.6 1.5 copy.6.mask
  2.1 140.2 %shard_map.59 = (bf16[256,1536]{1,0:T(8,128)(2,1)}, f32[16,16,128]{2,1,0:T(8,128)}) custom-call(bf16[1536,256]{1,0:T(8,128)(2,1)} %fac.1, bf16[1536,3072]{1,0:T(8,128)(2,1)} %a_hbm.1, s32[192,16]{1,0:T(8,128)} %copy.6.mask, f32[128,16,128]{2,1,0:T(8,128)} %bitcast.2), custom_call_target="tpu_custom_call" | custom-call | tf_op jit(solution)/shard_map/pallas_call | solution.py:515
  142.3 2.1 %copy.9 = bf16[256,1536]{1,0:T(8,128)(2,1)} copy(bf16[256,1536]{1,0:T(8,128)(2,1)} %get-tuple-element.8) | data formatting | bytes 1572864
  144.3 1.6 %copy.10 = f32[2,128,128]{2,1,0:T(8,128)} copy(f32[2,128,128]{2,1,0:T(8,128)} %bitcast.3) | data formatting | bytes 262144

commit v6 on v5

--- a/solution.py
+++ b/solution.py
@@ -12,7 +12,7 @@
 HALVES = 2
 SLOTS = 4
 PARTS = 3
-SHARES = ((4, 4, 4), (4, 4, 4), (4, 4, 4), (5, 5, 2))
+SHARES = ((5, 2, 5), (4, 4, 4), (4, 4, 4), (5, 5, 2))
 STEPS = SLOTS * PARTS
 
 PIECES = (4, 2)

time: 146 us -> 146 us (level)
  no operation moved by 1% of the time
where the time goes in v6:
time: 146 us; the launch traced here: 145 us
  Pallas kernels  140 us (96%)
  local copies, waits for them, and re-layouts  5.09 us (3%)
    pallas_call x1, Pallas kernels, per_device(): pl.pallas_call(kernel, out_shape=(jax.ShapeDtypeStruct((cols, rows), BF),...  140 us
    unnamed x3, local copies, waits for them, and re-layouts  5.09 us

profile of v6, /device:TPU:1, one launch (start us, length us, event | category | flops | bytes accessed | tf_op | source)
XLA Modules:
  0.0 145.5 jit_solution(1220019790111281619)
XLA Ops:
  0.6 1.5 %copy.6.mask = s32[192,16]{1,0:T(8,128)} copy(s32[192,16]{0,1:T(8,128)} %param.6) | data formatting | bytes 24576 | tf_op args[2]
  2.1 139.8 %shard_map.59 = (bf16[256,1536]{1,0:T(8,128)(2,1)}, f32[16,16,128]{2,1,0:T(8,128)}) custom-call(bf16[1536,256]{1,0:T(8,128)(2,1)} %fac.1, bf16[1536,3072]{1,0:T(8,128)(2,1)} %a_hbm.1, s32[192,16]{1,0:T(8,128)} %copy.6.mask, f32[128,16,128]{2,1,0:T(8,128)} %bitcast.2), custom_call_target="tpu_custom_call" | custom-call | tf_op jit(solution)/shard_map/pallas_call | solution.py:515
  141.8 2.1 %copy.9 = bf16[256,1536]{1,0:T(8,128)(2,1)} copy(bf16[256,1536]{1,0:T(8,128)(2,1)} %get-tuple-element.8) | data formatting | bytes 1572864
  143.9 1.6 %copy.10 = f32[2,128,128]{2,1,0:T(8,128)} copy(f32[2,128,128]{2,1,0:T(8,128)} %bitcast.3) | data formatting | bytes 262144
